TPU v7x, 128 devices: a whole 4x4x4 slice. The times are simulated.
128 devices in a mesh: dp: 4 (over y), tensor: 32 (over x, z, core).
Axes of the slice: x: 4, y: 4, z: 4, core: 2. Of those that a mesh axis runs over, the one named last changes fastest.
Arguments:
- tokens_in: bfloat16 [3072, 5120], P('dp', 'tensor')
- out_grad: bfloat16 [3072, 5120], P('dp', 'tensor'), may hold values from -6 to 6
- tenant: int32 [3072], P('dp'), may hold values from 0 to 32767, as said below
- slot_of: int32 [32768], replicated, may hold values from 0 to 32767, as said below
- steer_table: bfloat16 [32768, 5120], P(('dp', 'tensor')), may hold values from -6 to 6
- norm_gain: bfloat16 [5120], P('tensor'), may hold values from 0.099609375 to 1.8984375
- w_gate: bfloat16 [5120, 16384], P(None, 'tensor'), may hold values from -0.078125 to 0.078125
- w_up: bfloat16 [5120, 16384], P(None, 'tensor'), may hold values from -0.078125 to 0.078125
- w_down: bfloat16 [16384, 5120], P('tensor'), may hold values from -0.046875 to 0.046875
Outputs:
- input_grad: bfloat16 [3072, 5120], P('dp', 'tensor')
- table_grad: float32 [32768, 5120], P(('dp', 'tensor'))
Inputs may be any that keep to these rules, and one draw needn't show every extreme that they name: slot_of names every row of the table exactly once. `tenant`: in each aligned block of 768 tokens (one dp index), at most 24 tokens have tenants t with slot_of[t] // 256 equal to one value, and in every block some value is taken by exactly 24 tokens.
All inputs are finite; a program needn't handle non-finite values.
Results may differ from a plain program's by a relative error of at most 0.0065.
Values may be sent and summed in bfloat16 or wider, within the bound.
A program may use at most 128 MiB of HBM per device.

v0:
```python
import functools

import jax
import jax.numpy as jnp
from jax import lax
from jax.experimental import pallas as pl
from jax.experimental.pallas import tpu as pltpu
from jax.sharding import PartitionSpec as P

D = 5120
F32 = jnp.float32
BF16 = jnp.bfloat16


def dot(a, b, ca, cb):
    return lax.dot_general(a, b, (((ca,), (cb,)), ((), ())), preferred_element_type=F32)


def one_hot(index, size):
    return index[..., None] == jnp.arange(size, dtype=jnp.int32)


def look_up_slots(slot_of, tenant):
    lines = slot_of.reshape(-1, 128)
    halves = jnp.concatenate([lines // 256, lines % 256], axis=1).astype(BF16)
    picked = dot(one_hot(tenant // 128, lines.shape[0]).astype(BF16), halves, 1, 0)
    lane = one_hot(tenant % 128, 128)
    owners = jnp.sum(jnp.where(lane, picked[:, :128], 0.0), axis=1).astype(jnp.int32)
    rows = jnp.sum(jnp.where(lane, picked[:, 128:], 0.0), axis=1).astype(jnp.int32)
    return owners, rows


CHUNKS = 3
SIDE = 4
HALF = 80
KB = 640
AG_P1 = 0
AG_P2 = 6
AG_SIB = 12
RS_SIB = 20
RS_R1 = 24
RS_R2 = 30
DOT_SIB = 36
DOT_X = 37
DOT_Z = 40
SLOTS = 43


def core_kernel(
    res_ref, og_own_ref, gain_own_ref, og_hbm, wd_hbm, wg_hbm, wu_hbm, wgt_hbm, wut_hbm,
    out_ref,
    x_all, wg, wu, wgt, wut, gain, og_buf, wd_buf, hid, y_buf, g_acc, u_acc, both, inv_s,
    part, sib_in, ra, rb, rc, rst, rsum, qa, qb, qc, qst,
    dp_, ds, dq, dxf, dxb, dxo, dr, dzf, dzb, dzo,
    ssem, rsem, lsem, hsem,
):
    ten = lax.axis_index("tensor")
    x = ten // 8
    z = lax.rem(ten // 2, 4)
    c = lax.rem(ten, 2)
    step = 1 - 2 * c
    xf, xb, xo = lax.rem(x + step + 4, 4), lax.rem(x - step + 4, 4), lax.rem(x + 2, 4)
    zf, zb, zo = lax.rem(z + step + 4, 4), lax.rem(z - step + 4, 4), lax.rem(z + 2, 4)

    def dev(xx, zz, cc):
        return {"tensor": (xx * 4 + zz) * 2 + cc}

    to_xf, to_xb = dev(xf, z, c), dev(xb, z, c)
    to_zf, to_zb = dev(x, zf, c), dev(x, zb, c)
    to_sib = dev(x, z, 1 - c)
    width = res_ref.shape[1]
    tok = width // CHUNKS
    rows = SIDE * 2 * 2 * HALF

    local = [
        pltpu.make_async_copy(wgt_hbm, wgt, lsem.at[0]),
        pltpu.make_async_copy(wut_hbm, wut, lsem.at[1]),
        pltpu.make_async_copy(wg_hbm, wg, lsem.at[2]),
        pltpu.make_async_copy(wu_hbm, wu, lsem.at[3]),
        pltpu.make_async_copy(og_hbm.at[:, pl.ds(width, 128)], gain, lsem.at[4]),
    ]

    def hidden_copies(j):
        return (
            pltpu.make_async_copy(og_hbm.at[pl.ds(j * KB, KB), pl.ds(0, width)], og_buf.at[j % 2], hsem.at[0, j % 2]),
            pltpu.make_async_copy(wd_hbm.at[:, pl.ds(j * KB, KB)], wd_buf.at[j % 2], hsem.at[1, j % 2]),
        )

    for copy in hidden_copies(0) + hidden_copies(1):
        copy.start()
    for copy in local:
        copy.start()

    for k in range(CHUNKS):
        for h in range(2):
            x_all[k, x, z, c, h] = res_ref[h * HALF:(h + 1) * HALF, k * tok:(k + 1) * tok]

    barrier = pltpu.get_barrier_semaphore()
    for where in (to_xf, to_xb, to_zf, to_zb, to_sib):
        pl.semaphore_signal(barrier, inc=1, device_id=where, device_id_type=pl.DeviceIdType.MESH)
    pl.semaphore_wait(barrier, 5)

    sent = []

    def move(src, dst, k, slot, where):
        copy = pltpu.make_async_remote_copy(
            src_ref=src, dst_ref=dst, send_sem=ssem.at[k, slot], recv_sem=rsem.at[k, slot],
            device_id=where, device_id_type=pl.DeviceIdType.MESH,
        )
        copy.start()
        sent.append(copy)

    def arrived(dst, k, slot, where):
        pltpu.make_async_remote_copy(
            src_ref=dst, dst_ref=dst, send_sem=ssem.at[k, slot], recv_sem=rsem.at[k, slot],
            device_id=where, device_id_type=pl.DeviceIdType.MESH,
        ).wait_recv()

    def one(k, xx, zz, h):
        return x_all.at[k, xx, zz, c, h]

    def line(k, h, at, cc):
        return x_all.at[k, at, :, cc, 0] if h == 0 else x_all.at[k, :, at, cc, 1]

    near_to = ((to_zf, to_zb), (to_xf, to_xb))
    far_to = ((to_xf, to_xb), (to_zf, to_zb))
    far_at = ((x, xb, xf, xo), (z, zb, zf, zo))

    def near(k, h, at):
        return one(k, x, at, 0) if h == 0 else one(k, at, z, 1)

    near_at = ((z, zb, zf, zo), (x, xb, xf, xo))

    def ag1(k):
        for h in range(2):
            own = one(k, x, z, h)
            move(own, own, k, AG_P1 + 3 * h, near_to[h][0])
            move(own, own, k, AG_P1 + 3 * h + 1, near_to[h][1])

    def ag2(k):
        for h in range(2):
            behind = near(k, h, near_at[h][1])
            arrived(behind, k, AG_P1 + 3 * h, near_to[h][1])
            move(behind, behind, k, AG_P1 + 3 * h + 2, near_to[h][0])

    def ag3(k):
        for h in range(2):
            arrived(near(k, h, near_at[h][2]), k, AG_P1 + 3 * h + 1, near_to[h][0])
            arrived(near(k, h, near_at[h][3]), k, AG_P1 + 3 * h + 2, near_to[h][1])
            own = line(k, h, far_at[h][0], c)
            move(own, own, k, AG_P2 + 3 * h, far_to[h][0])
            move(own, own, k, AG_P2 + 3 * h + 1, far_to[h][1])
            move(own, own, k, AG_SIB + 4 * h, to_sib)

    def ag4(k):
        for h in range(2):
            behind = line(k, h, far_at[h][1], c)
            arrived(behind, k, AG_P2 + 3 * h, far_to[h][1])
            move(behind, behind, k, AG_P2 + 3 * h + 2, far_to[h][0])
            move(behind, behind, k, AG_SIB + 4 * h + 1, to_sib)
        for h in range(2):
            ahead = line(k, h, far_at[h][2], c)
            arrived(ahead, k, AG_P2 + 3 * h + 1, far_to[h][0])
            move(ahead, ahead, k, AG_SIB + 4 * h + 2, to_sib)

    def ag5(k):
        for h in range(2):
            opposite = line(k, h, far_at[h][3], c)
            arrived(opposite, k, AG_P2 + 3 * h + 2, far_to[h][1])
            move(opposite, opposite, k, AG_SIB + 4 * h + 3, to_sib)

    def ag6(k):
        for h in range(2):
            at = far_at[h]
            for n, i in enumerate((0, 2, 1, 3)):
                arrived(line(k, h, at[i], 1 - c), k, AG_SIB + 4 * h + n, to_sib)

    def hidden(j):
        for copy in hidden_copies(j):
            copy.wait()
        part_sum = jnp.dot(wd_buf[j % 2], og_buf[j % 2], preferred_element_type=F32)
        if j == 0:
            hid[...] = part_sum
        else:
            hid[...] += part_sum
        if j + 2 < D // KB:
            for copy in hidden_copies(j + 2):
                copy.start()

    def gates(k):
        g_acc[...] = jnp.zeros_like(g_acc)
        u_acc[...] = jnp.zeros_like(u_acc)

        def body(i, squares):
            at = pl.multiple_of(i * rows, rows)
            wide = x_all[k, i].reshape(rows, tok).astype(F32)
            scale = gain[pl.ds(at, rows), :].astype(F32)
            scale = jnp.concatenate([scale] * (tok // 128), axis=1)
            y_buf[...] = (wide * scale).astype(BF16)
            g_acc[...] += jnp.dot(wgt[:, pl.ds(at, rows)], y_buf[...], preferred_element_type=F32)
            u_acc[...] += jnp.dot(wut[:, pl.ds(at, rows)], y_buf[...], preferred_element_type=F32)
            return squares + jnp.sum(wide * wide, axis=0, keepdims=True)

        squares = lax.fori_loop(0, SIDE, body, jnp.zeros((1, tok), F32))
        inverse = lax.rsqrt(squares / D + 1e-06)
        inv_s[k] = jnp.broadcast_to(inverse, (8, tok))
        gate_out = g_acc[...] * inverse
        up_out = u_acc[...] * inverse
        hidden_grad = hid[:, k * tok:(k + 1) * tok]
        sigma = jax.nn.sigmoid(gate_out)
        gate_grad = (hidden_grad * up_out * (sigma * (1.0 + gate_out * (1.0 - sigma)))).astype(BF16)
        up_grad = (hidden_grad * (gate_out * sigma)).astype(BF16)
        half = gate_grad.shape[0]
        both[0:half] = gate_grad
        both[half:2 * half] = up_grad
        dots = jnp.sum(gate_grad.astype(F32) * gate_out + up_grad.astype(F32) * up_out, axis=0, keepdims=True)
        dp_[k] = jnp.broadcast_to(dots, (8, tok))
        move(dp_.at[k], dq.at[k], k, DOT_SIB, to_sib)

    def last(k):
        half = both.shape[0] // 2

        for i in range(SIDE):
            at = i * rows
            term = jnp.dot(wg[at:at + rows, :], both[0:half], preferred_element_type=F32)
            term = term + jnp.dot(wu[at:at + rows, :], both[half:2 * half], preferred_element_type=F32)
            part[k, i] = term.astype(BF16).reshape(SIDE, 2, 2, HALF, tok)
            move(part.at[k, i, :, 1 - c], sib_in.at[k, i], k, RS_SIB + i, to_sib)

    def add(*refs_):
        total = refs_[0].astype(F32)
        for other in refs_[1:]:
            total = total + other.astype(F32)
        return total

    def chip_line(k, h, at):
        return part.at[k, at, :, c, 0] if h == 0 else part.at[k, :, at, c, 1]

    def rs0(k):
        for i in range(SIDE):
            arrived(sib_in.at[k, i], k, RS_SIB + i, to_sib)
            part[k, i, :, c] = add(part[k, i, :, c], sib_in[k, i]).astype(BF16)
        for h in range(2):
            move(chip_line(k, h, far_at[h][3]), ra.at[k, h], k, RS_R1 + 3 * h, far_to[h][0])
        for h in range(2):
            move(chip_line(k, h, far_at[h][1]), rb.at[k, h], k, RS_R1 + 3 * h + 1, far_to[h][1])
        arrived(dq.at[k], k, DOT_SIB, to_sib)
        ds[k] = dp_[k] + dq[k]

    def rs0b(k):
        move(ds.at[k], dxf.at[k], k, DOT_X, to_xf)
        move(ds.at[k], dxb.at[k], k, DOT_X + 1, to_xb)

    def rs1(k):
        for h in range(2):
            arrived(ra.at[k, h], k, RS_R1 + 3 * h, far_to[h][1])
            rst[k, h] = add(ra[k, h], chip_line(k, h, far_at[h][2])[...]).astype(BF16)
            move(rst.at[k, h], rc.at[k, h], k, RS_R1 + 3 * h + 2, far_to[h][0])
        arrived(dxf.at[k], k, DOT_X, to_xb)
        move(dxf.at[k], dxo.at[k], k, DOT_X + 2, to_xf)

    def rs2(k):
        for h in range(2):
            arrived(rb.at[k, h], k, RS_R1 + 3 * h + 1, far_to[h][0])
            arrived(rc.at[k, h], k, RS_R1 + 3 * h + 2, far_to[h][1])
            rsum[k, h] = add(chip_line(k, h, far_at[h][0])[...], rb[k, h], rc[k, h]).astype(BF16)
            move(rsum.at[k, h, near_at[h][3]], qa.at[k, h], k, RS_R2 + 3 * h, near_to[h][0])
            move(rsum.at[k, h, near_at[h][1]], qb.at[k, h], k, RS_R2 + 3 * h + 1, near_to[h][1])
        arrived(dxb.at[k], k, DOT_X + 1, to_xf)
        arrived(dxo.at[k], k, DOT_X + 2, to_xb)
        dr[k] = ds[k] + dxf[k] + dxb[k] + dxo[k]
        move(dr.at[k], dzf.at[k], k, DOT_Z, to_zf)
        move(dr.at[k], dzb.at[k], k, DOT_Z + 1, to_zb)

    def rs3(k):
        for h in range(2):
            arrived(qa.at[k, h], k, RS_R2 + 3 * h, near_to[h][1])
            qst[k, h] = add(qa[k, h], rsum[k, h, near_at[h][2]]).astype(BF16)
            move(qst.at[k, h], qc.at[k, h], k, RS_R2 + 3 * h + 2, near_to[h][0])
        arrived(dzf.at[k], k, DOT_Z, to_zb)
        move(dzf.at[k], dzo.at[k], k, DOT_Z + 2, to_zf)

    def rs4(k):
        arrived(dzb.at[k], k, DOT_Z + 1, to_zf)
        arrived(dzo.at[k], k, DOT_Z + 2, to_zb)
        dots = (dr[k] + dzf[k] + dzb[k] + dzo[k])[0:1]
        inverse = inv_s[k][0:1]
        pull = dots * inverse * inverse / D
        for h in range(2):
            arrived(qb.at[k, h], k, RS_R2 + 3 * h + 1, near_to[h][0])
            arrived(qc.at[k, h], k, RS_R2 + 3 * h + 2, near_to[h][1])
            norm_grad = add(rsum[k, h, near_at[h][0]], qb[k, h], qc[k, h])
            span = slice(h * HALF, (h + 1) * HALF)
            cols = slice(k * tok, (k + 1) * tok)
            full = og_own_ref[span, cols].astype(F32) + gain_own_ref[span, 0:1].astype(F32) * inverse * norm_grad
            full = full - res_ref[span, cols].astype(F32) * pull
            out_ref[span, cols] = full.astype(BF16)

    def wait_local(*which):
        for n in which:
            local[n].wait()

    for k in range(CHUNKS):
        ag1(k)
    hidden(0)
    ag2(0)
    hidden(1)
    ag3(0)
    ag2(1)
    hidden(2)
    ag3(1)
    ag2(2)
    hidden(3)
    ag4(0)
    hidden(4)
    ag3(2)
    hidden(5)
    ag5(0)
    hidden(6)
    ag4(1)
    hidden(7)
    wait_local(4, 0, 1)
    ag6(0)
    gates(0)
    ag5(1)
    ag4(2)
    wait_local(2, 3)
    last(0)
    ag6(1)
    gates(1)
    rs0(0)
    rs0b(0)
    ag5(2)
    last(1)
    rs1(0)
    ag6(2)
    gates(2)
    rs2(0)
    rs0(1)
    rs0b(1)
    last(2)
    rs3(0)
    rs1(1)
    rs4(0)
    rs0(2)
    rs0b(2)
    rs2(1)
    rs3(1)
    rs1(2)
    rs4(1)
    rs2(2)
    rs3(2)
    rs4(2)
    for copy in sent:
        copy.wait_send()


def core(residual, out_grad_t, gain_own, og_ext, w_down, w_gate, w_up):
    width = residual.shape[1]
    tok = width // CHUNKS
    hid = w_gate.shape[1]
    vm = pl.BlockSpec(memory_space=pltpu.VMEM)
    hbm = pl.BlockSpec(memory_space=pl.ANY)

    def bf(*shape):
        return pltpu.VMEM(shape, BF16)

    def fl(*shape):
        return pltpu.VMEM(shape, F32)

    rows = SIDE * 2 * 2 * HALF
    return pl.pallas_call(
        core_kernel,
        out_shape=jax.ShapeDtypeStruct(residual.shape, BF16),
        in_specs=[vm] * 3 + [hbm] * 6,
        out_specs=vm,
        scratch_shapes=[
            bf(CHUNKS, SIDE, SIDE, 2, 2, HALF, tok),
            bf(D, hid), bf(D, hid), bf(hid, D), bf(hid, D),
            bf(D, 128),
            bf(2, KB, width), bf(2, hid, KB),
            fl(hid, width),
            bf(rows, tok), fl(hid, tok), fl(hid, tok), bf(2 * hid, tok), fl(CHUNKS, 8, tok),
            bf(CHUNKS, SIDE, SIDE, 2, 2, HALF, tok), bf(CHUNKS, SIDE, SIDE, 2, HALF, tok),
        ]
        + [bf(CHUNKS, 2, SIDE, HALF, tok)] * 5
        + [bf(CHUNKS, 2, HALF, tok)] * 4
        + [fl(CHUNKS, 8, tok)] * 10
        + [
            pltpu.SemaphoreType.DMA((CHUNKS, SLOTS)),
            pltpu.SemaphoreType.DMA((CHUNKS, SLOTS)),
            pltpu.SemaphoreType.DMA((5,)),
            pltpu.SemaphoreType.DMA((2, 2)),
        ],
        compiler_params=pltpu.CompilerParams(
            collective_id=0, has_side_effects=True, vmem_limit_bytes=60 * 1024 * 1024
        ),
        cost_estimate=pl.CostEstimate(flops=10 * D * hid * width, bytes_accessed=40_000_000, transcendentals=0),
        name="core",
    )(residual, out_grad_t, gain_own, og_ext, w_down, w_gate, w_up, w_gate.T, w_up.T)


def per_device(tokens_in, out_grad, tenant, slot_of, steer_table, norm_gain, w_gate, w_up, w_down):
    holders = lax.axis_size(("dp", "tensor"))
    groups = lax.axis_size("dp")
    width_parts = lax.axis_size("tensor")
    rows_own = steer_table.shape[0]
    feat_local = tokens_in.shape[1]
    token_count = tenant.shape[0]
    capacity = 4 * token_count // holders
    group = lax.axis_index("dp")
    me = lax.axis_index(("dp", "tensor"))

    tenant_all = lax.all_gather(tenant, "dp", axis=0, tiled=True)
    out_grad_t = out_grad.T
    gain_own = jnp.broadcast_to(norm_gain[:, None], (feat_local, 128))
    og_ext = lax.all_gather(jnp.concatenate([out_grad_t, gain_own], axis=1), "tensor", axis=0, tiled=True)

    owners_all, rows_all = look_up_slots(slot_of, tenant_all)
    earlier = (
        jnp.arange(token_count, dtype=jnp.int32)[:, None] < jnp.arange(token_count, dtype=jnp.int32)[None, :]
    ).astype(BF16)
    mine = (owners_all == me).reshape(groups, token_count)
    rank_mine = dot(mine.astype(BF16), earlier, 1, 0).astype(jnp.int32)
    slot_of_token = jnp.where(mine, rank_mine, -1)
    slots = (slot_of_token[:, None, :] == jnp.arange(capacity, dtype=jnp.int32)[None, :, None]).astype(BF16)
    row_hot = one_hot(rows_all.reshape(groups, token_count), rows_own).astype(BF16)
    wanted = lax.dot_general(slots, row_hot, (((2,), (1,)), ((0,), (0,))), preferred_element_type=F32)
    wanted = wanted.astype(BF16).reshape(groups * capacity, rows_own)
    picked = dot(wanted, steer_table, 1, 0).astype(BF16)
    outgoing = picked.reshape(groups, capacity, width_parts, feat_local).transpose(0, 2, 1, 3)
    outgoing = outgoing.reshape(holders, capacity, feat_local)
    returned = lax.all_to_all(outgoing, ("dp", "tensor"), split_axis=0, concat_axis=0, tiled=True)
    returned = returned.reshape(holders * capacity, feat_local)

    owners = lax.dynamic_slice_in_dim(owners_all, group * token_count, token_count)
    matches = one_hot(owners, holders).astype(BF16)
    before = dot(earlier, matches, 0, 0)
    ranking = jnp.sum(jnp.where(matches > 0, before, 0.0), axis=1).astype(jnp.int32)
    place = one_hot(owners * capacity + ranking, holders * capacity).astype(BF16)
    steering = dot(returned, place, 0, 1)

    residual = (tokens_in.T.astype(F32) + steering).astype(BF16)
    full_grad = core(residual, out_grad_t, gain_own, og_ext, w_down, w_gate, w_up)

    sending = dot(place, full_grad, 0, 1).astype(BF16).reshape(holders, capacity, feat_local)
    received = lax.all_to_all(sending, ("dp", "tensor"), split_axis=0, concat_axis=0, tiled=True)
    received = received.reshape(groups, width_parts, capacity, feat_local).transpose(0, 2, 1, 3)
    received = received.reshape(groups * capacity, width_parts * feat_local)
    table_grad = dot(wanted, received, 0, 0)
    return (full_grad.T, table_grad)


def solution(mesh):
    placed = (
        P("dp", "tensor"),
        P("dp", "tensor"),
        P("dp"),
        P(),
        P(("dp", "tensor"), None),
        P("tensor"),
        P(None, "tensor"),
        P(None, "tensor"),
        P("tensor", None),
    )
    return jax.shard_map(
        per_device,
        mesh=mesh,
        in_specs=placed,
        out_specs=(P("dp", "tensor"), P(("dp", "tensor"), None)),
        check_vma=False,
    )
```

profile of v0, /device:TPU:1, one launch (start us, length us, event | category | flops | bytes accessed | tf_op | source)
XLA Modules:
  0.0 230.2 jit_solution(11838159223554768636)
XLA Ops:
  7.2 0.9 broadcast_in_dim.17.gain_own_ref
  8.1 1.7 pad_maximum_fusion
  9.8 0.7 reshape.53
  10.5 10.3 %all-gather = s32[4,1,768]{2,1,0:T(1,128)S(1)} all-gather(s32[1,1,768]{2,1,0:T(1,128)S(1)} %reshape.53), channel_id=1, replica_groups=mesh['dp'=4,'tensor'=32] {'dp'}, dimensions={0}, use_global_device_ids=true | all-gather | bytes 15360 | tf_op jit(solution)/shard_map/all_gather | solution.py:414
  20.9 1.0 fusion.23
  21.9 0.9 fusion.5
  23.4 0.9 fusion.17
  24.3 1.5 convolution_convert_fusion
  25.8 4.0 %reshape.47 = bf16[4,24,32,160]{3,2,1,0:T(8,128)(2,1)} reshape(bf16[96,5120]{1,0:T(8,128)(2,1)} %convolution_convert_fusion) | data formatting | bytes 1966080 | tf_op jit(solution)/shard_map/reshape | solution.py:431
  29.8 3.4 %copy.18 = bf16[4,24,32,160]{3,1,2,0:T(8,128)(2,1)} copy(bf16[4,24,32,160]{3,2,1,0:T(8,128)(2,1)} %reshape.47) | data formatting | bytes 1966080 | tf_op jit(solution)/shard_map/reshape | solution.py:431
  33.3 13.2 %all-to-all-start = ((bf16[128,24,160]{2,1,0:T(8,128)(2,1)}), bf16[128,24,160]{2,1,0:T(8,128)(2,1)}, u32[]{:S(2)}, u32[]{:S(2)}) async-start(bf16[128,24,160]{2,1,0:T(8,128)(2,1)} %bitcast.52), calls=%async_computation | async-start | bytes 3145728 | tf_op jit(solution)/shard_map/all_to_all | solution.py:433
  46.5 7.9 %copy.19 = bf16[5120,512]{0,1:T(8,128)(2,1)} copy(bf16[5120,512]{1,0:T(8,128)(2,1)} %wg_hbm.1) | data formatting | bytes 10485760 | tf_op args[6]
  54.4 8.0 %copy.20 = bf16[5120,512]{0,1:T(8,128)(2,1)} copy(bf16[5120,512]{1,0:T(8,128)(2,1)} %wu_hbm.1) | data formatting | bytes 10485760 | tf_op args[7]
  63.0 23.2 %all-to-all-done = bf16[128,24,160]{2,1,0:T(8,128)(2,1)} async-done(((bf16[128,24,160]{2,1,0:T(8,128)(2,1)}), bf16[128,24,160]{2,1,0:T(8,128)(2,1)}, u32[]{:S(2)}, u32[]{:S(2)}) %all-to-all-start) | async-done | bytes 983072 | tf_op jit(solution)/shard_map/all_to_all | solution.py:433
  86.2 4.1 %fusion.15.res_ref = bf16[160,768]{1,0:T(8,128)(2,1)} fusion(bf16[3072,160]{1,0:T(8,128)(2,1)} %bitcast.6, s32[768]{0:T(1024)S(1)} %convert_add_fusion, bf16[768,160]{0,1:T(8,128)(2,1)S(1)} %copy-done.3), kind=kOutput, calls=%fused_computation.24 | convolution fusion | flops 757702656 | bytes 1477632 | tf_op jit(solution)/shard_map/dot_general | solution.py:16
  90.3 78.9 %core.1 = bf16[160,768]{1,0:T(8,128)(2,1)} custom-call(bf16[160,768]{1,0:T(8,128)(2,1)} %fusion.15.res_ref, bf16[160,768]{1,0:T(8,128)(2,1)} %bitcast.58, bf16[160,128]{1,0:T(8,128)(2,1)} %copy-done.2, bf16[5120,896]{1,0:T(8,128)(2,1)} %all-gather.3.cloned.1.call-done.og_hbm, bf16[512,5120]{1,0:T(8,128)(2,1)} %wd_hbm.1, bf16[5120,512]{1,0:T(8,128)(2,1)} %wg_hbm.1, ...), custom_call_target="tpu_custom_call" | custom-call | flops 20132659200 | bytes 40000000 | tf_op jit(solution)/shard_map/core/pallas_call | solution.py:372
  169.2 4.0 %fusion.4 = bf16[3072,160]{0,1:T(8,128)(2,1)} fusion(bf16[160,768]{1,0:T(8,128)(2,1)} %core.1, s32[768]{0:T(1024)S(1)} %convert_add_fusion), kind=kOutput, calls=%fused_computation.6 | convolution fusion | flops 757825536 | bytes 1231872 | tf_op jit(solution)/shard_map/dot_general | solution.py:16
  173.3 2.5 %copy.21 = bf16[3072,160]{1,0:T(8,128)(2,1)} copy(bf16[3072,160]{0,1:T(8,128)(2,1)} %fusion.4) | data formatting | bytes 1966080 | tf_op jit(solution)/shard_map/convert_element_type | solution.py:446
  175.7 11.0 %all-to-all-start.1 = ((bf16[128,24,160]{2,1,0:T(8,128)(2,1)}), bf16[128,24,160]{2,1,0:T(8,128)(2,1)}, u32[]{:S(2)}, u32[]{:S(2)}) async-start(bf16[128,24,160]{2,1,0:T(8,128)(2,1)} %bitcast.53), calls=%async_computation.1 | async-start | bytes 3145728 | tf_op jit(solution)/shard_map/all_to_all | solution.py:447
  186.7 24.4 %all-to-all-done.1 = bf16[128,24,160]{2,1,0:T(8,128)(2,1)} async-done(((bf16[128,24,160]{2,1,0:T(8,128)(2,1)}), bf16[128,24,160]{2,1,0:T(8,128)(2,1)}, u32[]{:S(2)}, u32[]{:S(2)}) %all-to-all-start.1) | async-done | bytes 983072 | tf_op jit(solution)/shard_map/all_to_all | solution.py:447
  211.1 2.9 %copy.24 = bf16[4,32,24,160]{3,1,2,0:T(8,128)(2,1)} copy(bf16[4,32,24,160]{3,2,1,0:T(8,128)(2,1)} %bitcast.12) | data formatting | bytes 1966080 | tf_op jit(solution)/shard_map/reshape | solution.py:448
  214.0 4.2 %reshape.52 = bf16[96,5120]{1,0:T(8,128)(2,1)} reshape(bf16[4,24,32,160]{3,2,1,0:T(8,128)(2,1)} %bitcast.54) | data formatting | bytes 1966080 | tf_op jit(solution)/shard_map/reshape | solution.py:449
  218.2 4.5 %fusion.34 = f32[256,5120]{1,0:T(8,128)} fusion(bf16[96,256]{1,0:T(8,128)(2,1)S(1)} %bitcast.61, bf16[96,5120]{1,0:T(8,128)(2,1)} %reshape.52), kind=kOutput, calls=%fused_computation.61 | convolution fusion | flops 251658240 | bytes 6275072 | tf_op jit(solution)/shard_map/dot_general | solution.py:16
  222.7 0.7 copy.26
  (22 shorter events, 1.2 us)
Async XLA Ops:
  7.2 17.1 %copy-start = (bf16[256,5120]{1,0:T(8,128)(2,1)S(1)}, bf16[256,5120]{1,0:T(8,128)(2,1)}, u32[]{:S(2)}) copy-start(bf16[256,5120]{1,0:T(8,128)(2,1)} %param.13) | copy-start | bytes 7864324
  7.2 83.1 %all-gather.3.cloned.1.call-start = ((), (), s32[]{:S(2)}) async-start(), calls=%async_computation.2 | async-start | bytes 9461760 | tf_op jit(solution)/shard_map/all_gather | solution.py:417
  8.1 14.6 %copy-start.2 = (bf16[160,128]{1,0:T(8,128)(2,1)}, bf16[160,128]{1,0:T(8,128)(2,1)S(1)}, u32[]{:S(2)}) copy-start(bf16[160,128]{1,0:T(8,128)(2,1)S(1)} %broadcast_in_dim.17.gain_own_ref) | copy-start | bytes 122884
  33.3 52.9 %all-to-all-start = ((bf16[128,24,160]{2,1,0:T(8,128)(2,1)}), bf16[128,24,160]{2,1,0:T(8,128)(2,1)}, u32[]{:S(2)}, u32[]{:S(2)}) async-start(bf16[128,24,160]{2,1,0:T(8,128)(2,1)} %bitcast.52), calls=%async_computation | async-start | bytes 3145728 | tf_op jit(solution)/shard_map/all_to_all | solution.py:433
  54.4 31.8 %copy-start.3 = (bf16[768,160]{0,1:T(8,128)(2,1)S(1)}, bf16[768,160]{0,1:T(8,128)(2,1)}, u32[]{:S(2)}) copy-start(bf16[768,160]{0,1:T(8,128)(2,1)} %param.9) | copy-start | bytes 737284
  175.7 35.4 %all-to-all-start.1 = ((bf16[128,24,160]{2,1,0:T(8,128)(2,1)}), bf16[128,24,160]{2,1,0:T(8,128)(2,1)}, u32[]{:S(2)}, u32[]{:S(2)}) async-start(bf16[128,24,160]{2,1,0:T(8,128)(2,1)} %bitcast.53), calls=%async_computation.1 | async-start | bytes 3145728 | tf_op jit(solution)/shard_map/all_to_all | solution.py:447
  218.2 4.5 %copy-start.1 = (bf16[160,768]{1,0:T(8,128)(2,1)S(1)}, bf16[160,768]{1,0:T(8,128)(2,1)}, u32[]{:S(2)}) copy-start(bf16[160,768]{1,0:T(8,128)(2,1)} %core.1) | copy-start | bytes 737284
Sparse Core Ops, SparseCore 0:
  10.3 75.0 all-gather.2
where the time goes:
time: 231 us; the launch traced here: 230 us
  Pallas kernels  78.9 us (34%)
  waiting for transfers between devices  47.6 us (21%)
  local copies, waits for them, and re-layouts  35.5 us (15%)
  starting transfers between devices  24.2 us (10%)
  matrix products  16.4 us (7%)
  between operations  14.2 us (6%)
  blocking collectives  10.3 us (4%)
  other arithmetic  3.18 us (1%)
    pallas_call x1, Pallas kernels, core(): pl.pallas_call(core_kernel, out_shape=jax.ShapeDtypeStruct(residual.shape...  78.9 us
    all_to_all x1, waiting for transfers between devices, per_device(): lax.all_to_all(sending, ('dp', 'tensor'), split_axis=0, concat_axis=0, ti...  24.4 us
    all_to_all x1, waiting for transfers between devices, per_device(): lax.all_to_all(outgoing, ('dp', 'tensor'), split_axis=0, concat_axis=0, t...  23.2 us
    unnamed x12, local copies, waits for them, and re-layouts  17.4 us
    dot_general x7, matrix products, dot(): lax.dot_general(a, b, (((ca,), (cb,)), ((), ())), preferred_element_type=...  15.5 us
    all_to_all x1, starting transfers between devices, per_device(): lax.all_to_all(outgoing, ('dp', 'tensor'), split_axis=0, concat_axis=0, t...  13.2 us
    all_to_all x1, starting transfers between devices, per_device(): lax.all_to_all(sending, ('dp', 'tensor'), split_axis=0, concat_axis=0, ti...  11 us
    all_gather x1, blocking collectives, per_device(): tenant_all = lax.all_gather(tenant, 'dp', axis=0, tiled=True)  10.3 us
  transfers between devices with their start and end apart: 3, of which 2 were waited for; matrix products, arithmetic and copies ran while one was open for 15% of the time, Pallas kernels for 0%

commit v1 on v0

--- a/solution.py
+++ b/solution.py
@@ -10,24 +10,6 @@
 D = 5120
 F32 = jnp.float32
 BF16 = jnp.bfloat16
-
-
-def dot(a, b, ca, cb):
-    return lax.dot_general(a, b, (((ca,), (cb,)), ((), ())), preferred_element_type=F32)
-
-
-def one_hot(index, size):
-    return index[..., None] == jnp.arange(size, dtype=jnp.int32)
-
-
-def look_up_slots(slot_of, tenant):
-    lines = slot_of.reshape(-1, 128)
-    halves = jnp.concatenate([lines // 256, lines % 256], axis=1).astype(BF16)
-    picked = dot(one_hot(tenant // 128, lines.shape[0]).astype(BF16), halves, 1, 0)
-    lane = one_hot(tenant % 128, 128)
-    owners = jnp.sum(jnp.where(lane, picked[:, :128], 0.0), axis=1).astype(jnp.int32)
-    rows = jnp.sum(jnp.where(lane, picked[:, 128:], 0.0), axis=1).astype(jnp.int32)
-    return owners, rows
 
 
 CHUNKS = 3
@@ -400,54 +382,423 @@
     )(residual, out_grad_t, gain_own, og_ext, w_down, w_gate, w_up, w_gate.T, w_up.T)
 
 
+MESH = pl.DeviceIdType.MESH
+SLOT = 32
+SPANS = ((0, 512), (512, 384))
+
+
+def nt(a, b):
+    return lax.dot_general(a, b, (((1,), (1,)), ((), ())), preferred_element_type=F32)
+
+
+def fetch_kernel(
+    tok_ref, og_ref, ten_ref, halves_ref, table_ref,
+    res_ref, og_out, wanted_ref, place_ref,
+    tbuf, earlier, rows_s, rows_r, turned, landed, acc,
+    tsend, trecv, ysend, yrecv, psend, precv, gsend, grecv, lsem,
+):
+    d = lax.axis_index("dp")
+    t = lax.axis_index("tensor")
+    me = d * 32 + t
+    x = t // 8
+    z = lax.rem(t // 2, 4)
+    c = lax.rem(t, 2)
+    step = 1 - 2 * c
+    xf, xb, xo = lax.rem(x + step + 4, 4), lax.rem(x - step + 4, 4), lax.rem(x + 2, 4)
+    zf, zb, zo = lax.rem(z + step + 4, 4), lax.rem(z - step + 4, 4), lax.rem(z + 2, 4)
+
+    def dev(xx, zz, cc):
+        return {"dp": d, "tensor": (xx * 4 + zz) * 2 + cc}
+
+    to_xf, to_xb = dev(xf, z, c), dev(xb, z, c)
+    to_zf, to_zb = dev(x, zf, c), dev(x, zb, c)
+    to_sib = dev(x, z, 1 - c)
+    width = tok_ref.shape[1]
+    feat = tok_ref.shape[0]
+    parts = D // feat
+
+    own_copies = [
+        pltpu.make_async_copy(og_ref.at[pl.ds(h * HALF, HALF)], og_out.at[x, z, c, h], lsem.at[h]) for h in range(2)
+    ]
+    for copy in own_copies:
+        copy.start()
+    barrier = pltpu.get_barrier_semaphore()
+
+    def greet(o, carry):
+        pl.semaphore_signal(
+            barrier, inc=1, device_id={"dp": d, "tensor": lax.rem(t + o, parts)}, device_id_type=MESH
+        )
+        return carry
+
+    lax.fori_loop(1, parts, greet, 0)
+    for o in (1, 2, 3):
+        pl.semaphore_signal(barrier, inc=1, device_id={"dp": lax.rem(d + o, 4), "tensor": t}, device_id_type=MESH)
+    pl.semaphore_wait(barrier, parts - 1 + 3)
+
+    sent = []
+
+    def send(src, dst, ssem, rsem, where):
+        copy = pltpu.make_async_remote_copy(
+            src_ref=src, dst_ref=dst, send_sem=ssem, recv_sem=rsem, device_id=where, device_id_type=MESH
+        )
+        copy.start()
+        sent.append(copy)
+
+    def got(dst, ssem, rsem, where):
+        pltpu.make_async_remote_copy(
+            src_ref=dst, dst_ref=dst, send_sem=ssem, recv_sem=rsem, device_id=where, device_id_type=MESH
+        ).wait_recv()
+
+    for o in (1, 3, 2):
+        there = lax.rem(d + o, 4)
+        send(ten_ref, tbuf.at[d], tsend.at[there], trecv.at[d], {"dp": there, "tensor": t})
+
+    near_to = ((to_zf, to_zb), (to_xf, to_xb))
+    far_to = ((to_xf, to_xb), (to_zf, to_zb))
+    near_at = ((z, zb, zf, zo), (x, xb, xf, xo))
+    far_at = ((x, xb, xf, xo), (z, zb, zf, zo))
+
+    def lanes(k):
+        return pl.ds(SPANS[k][0], SPANS[k][1])
+
+    def near(k, h, at):
+        return og_out.at[x, at, c, 0, :, lanes(k)] if h == 0 else og_out.at[at, z, c, 1, :, lanes(k)]
+
+    def line(k, h, at, cc):
+        return og_out.at[at, :, cc, 0, :, lanes(k)] if h == 0 else og_out.at[:, at, cc, 1, :, lanes(k)]
+
+    def move(src, dst, k, slot, where):
+        send(src, dst, gsend.at[k, slot], grecv.at[k, slot], where)
+
+    def arrived(dst, k, slot, where):
+        got(dst, gsend.at[k, slot], grecv.at[k, slot], where)
+
+    def ag1(k):
+        for h in range(2):
+            own = near(k, h, near_at[h][0])
+            src = og_ref.at[pl.ds(h * HALF, HALF), lanes(k)]
+            move(src, own, k, AG_P1 + 3 * h, near_to[h][0])
+            move(src, own, k, AG_P1 + 3 * h + 1, near_to[h][1])
+
+    def ag2(k):
+        for h in range(2):
+            behind = near(k, h, near_at[h][1])
+            arrived(behind, k, AG_P1 + 3 * h, near_to[h][1])
+            move(behind, behind, k, AG_P1 + 3 * h + 2, near_to[h][0])
+
+    def ag3(k):
+        for h in range(2):
+            arrived(near(k, h, near_at[h][2]), k, AG_P1 + 3 * h + 1, near_to[h][0])
+            arrived(near(k, h, near_at[h][3]), k, AG_P1 + 3 * h + 2, near_to[h][1])
+            own = line(k, h, far_at[h][0], c)
+            move(own, own, k, AG_P2 + 3 * h, far_to[h][0])
+            move(own, own, k, AG_P2 + 3 * h + 1, far_to[h][1])
+            move(own, own, k, AG_SIB + 4 * h, to_sib)
+
+    def ag4(k):
+        for h in range(2):
+            behind = line(k, h, far_at[h][1], c)
+            arrived(behind, k, AG_P2 + 3 * h, far_to[h][1])
+            move(behind, behind, k, AG_P2 + 3 * h + 2, far_to[h][0])
+            move(behind, behind, k, AG_SIB + 4 * h + 1, to_sib)
+        for h in range(2):
+            ahead = line(k, h, far_at[h][2], c)
+            arrived(ahead, k, AG_P2 + 3 * h + 1, far_to[h][0])
+            move(ahead, ahead, k, AG_SIB + 4 * h + 2, to_sib)
+
+    def ag5(k):
+        for h in range(2):
+            opposite = line(k, h, far_at[h][3], c)
+            arrived(opposite, k, AG_P2 + 3 * h + 2, far_to[h][1])
+            move(opposite, opposite, k, AG_SIB + 4 * h + 3, to_sib)
+
+    def ag6(k):
+        for h in range(2):
+            for n, i in enumerate((0, 2, 1, 3)):
+                arrived(line(k, h, far_at[h][i], 1 - c), k, AG_SIB + 4 * h + n, to_sib)
+
+    ag1(0)
+    ag1(1)
+
+    lines = halves_ref.shape[1]
+    earlier[...] = (
+        lax.broadcasted_iota(jnp.int32, (width, width), 0) < lax.broadcasted_iota(jnp.int32, (width, width), 1)
+    ).astype(F32).astype(BF16)
+
+    def hot(index, size):
+        return (lax.broadcasted_iota(jnp.int32, (size, width), 0) == index).astype(F32)
+
+    def look_up(tenant):
+        picked = jnp.dot(halves_ref[...], hot(tenant // 128, lines).astype(BF16), preferred_element_type=F32)
+        lane = hot(lax.rem(tenant, 128), 128)
+        owner = jnp.sum(lane * picked[:128], axis=0, keepdims=True).astype(jnp.int32)
+        row = jnp.sum(lane * picked[128:], axis=0, keepdims=True).astype(jnp.int32)
+        return owner, row
+
+    def ranks(matches):
+        before = jnp.dot(matches.astype(BF16), earlier[...], preferred_element_type=F32)
+        return jnp.sum(matches * before, axis=0, keepdims=True).astype(jnp.int32)
+
+    owner, row = look_up(ten_ref[0:1])
+    rank = ranks(hot(owner, 128))
+    place = lax.rem(owner, 32) * 128 + owner // 32 * SLOT + rank
+    place_ref[...] = jnp.broadcast_to(place, place_ref.shape)
+    ag2(0)
+    ag2(1)
+
+    tbuf[d] = ten_ref[...]
+    for o in (1, 3, 2):
+        there = lax.rem(d + o, 4)
+        got(tbuf.at[there], tsend.at[there], trecv.at[there], {"dp": there, "tensor": t})
+    for g in range(4):
+        owner, row = look_up(tbuf[g, 0:1])
+        mine = (owner == me).astype(F32)
+        mine8 = jnp.broadcast_to(mine, (8, width))
+        before = jnp.dot(mine8.astype(BF16), earlier[...], preferred_element_type=F32)[0:1]
+        slot = jnp.where(mine > 0, before.astype(jnp.int32), -1)
+        wanted = nt(hot(slot, SLOT).astype(BF16), hot(row, table_ref.shape[0]).astype(BF16)).astype(BF16)
+        wanted_ref[g * SLOT:(g + 1) * SLOT] = wanted
+        rows_s[g] = jnp.dot(wanted, table_ref[...], preferred_element_type=F32).astype(BF16)
+    for o in (1, 3, 2):
+        there = lax.rem(d + o, 4)
+        send(rows_s.at[there], rows_r.at[d], ysend.at[there], yrecv.at[d], {"dp": there, "tensor": t})
+    rows_r[d] = rows_s[d]
+    for copy in own_copies:
+        copy.wait()
+    ag3(0)
+    ag3(1)
+    ag4(0)
+    for o in (3, 1, 2):
+        there = lax.rem(d + o, 4)
+        got(rows_r.at[there], ysend.at[there], yrecv.at[there], {"dp": there, "tensor": t})
+    wide = 640
+
+    def turn(i, carry):
+        at = pl.multiple_of(i * wide, wide)
+        block = rows_r[:, :, pl.ds(at, wide)].reshape(4 * SLOT, wide)
+        turned[pl.ds(at, wide), :] = block.T
+        return carry
+
+    lax.fori_loop(0, D // wide, turn, 0)
+
+    def scatter(o, carry):
+        there = lax.rem(t + o, parts)
+        pltpu.make_async_remote_copy(
+            src_ref=turned.at[pl.ds(pl.multiple_of(there * feat, 16), feat)], dst_ref=landed.at[t],
+            send_sem=psend.at[there], recv_sem=precv.at[t],
+            device_id={"dp": d, "tensor": there}, device_id_type=MESH,
+        ).start()
+        return carry
+
+    lax.fori_loop(1, parts, scatter, 0)
+    landed[t] = turned[pl.ds(pl.multiple_of(t * feat, 16), feat), :]
+    acc[...] = tok_ref[...].astype(F32)
+    ag4(1)
+    ag5(0)
+
+    def add_from(src):
+        sel = (lax.broadcasted_iota(jnp.int32, (128, width), 0) + src * 128 == place).astype(F32).astype(BF16)
+        acc[...] += jnp.dot(landed[src], sel, preferred_element_type=F32)
+
+    add_from(t)
+
+    def gather(o, carry):
+        src = lax.rem(t + parts - o, parts)
+        pltpu.make_async_remote_copy(
+            src_ref=landed.at[src], dst_ref=landed.at[src],
+            send_sem=psend.at[src], recv_sem=precv.at[src],
+            device_id={"dp": d, "tensor": src}, device_id_type=MESH,
+        ).wait_recv()
+        add_from(src)
+        return carry
+
+    lax.fori_loop(1, parts, gather, 0)
+    res_ref[...] = acc[...].astype(BF16)
+    ag5(1)
+    ag6(0)
+    ag6(1)
+
+    def drain(o, carry):
+        there = lax.rem(t + o, parts)
+        pltpu.make_async_remote_copy(
+            src_ref=turned.at[pl.ds(pl.multiple_of(there * feat, 16), feat)], dst_ref=landed.at[t],
+            send_sem=psend.at[there], recv_sem=precv.at[t],
+            device_id={"dp": d, "tensor": there}, device_id_type=MESH,
+        ).wait_send()
+        return carry
+
+    lax.fori_loop(1, parts, drain, 0)
+    for copy in sent:
+        copy.wait_send()
+
+
+def fetch(tokens_t, og_ext, tenant8, halves, table):
+    feat, width = tokens_t.shape
+    parts = D // feat
+    vm = pl.BlockSpec(memory_space=pltpu.VMEM)
+    dma = pltpu.SemaphoreType.DMA
+    return pl.pallas_call(
+        fetch_kernel,
+        out_shape=(
+            jax.ShapeDtypeStruct((feat, width), BF16),
+            jax.ShapeDtypeStruct((SIDE, SIDE, 2, 2, HALF, og_ext.shape[1]), BF16),
+            jax.ShapeDtypeStruct((4 * SLOT, table.shape[0]), BF16),
+            jax.ShapeDtypeStruct((8, width), jnp.int32),
+        ),
+        in_specs=[vm] * 5,
+        out_specs=(vm, pl.BlockSpec(memory_space=pl.ANY), vm, vm),
+        scratch_shapes=[
+            pltpu.VMEM((4, 8, width), jnp.int32),
+            pltpu.VMEM((width, width), BF16),
+            pltpu.VMEM((4, SLOT, D), BF16),
+            pltpu.VMEM((4, SLOT, D), BF16),
+            pltpu.VMEM((D, 4 * SLOT), BF16),
+            pltpu.VMEM((parts, feat, 4 * SLOT), BF16),
+            pltpu.VMEM((feat, width), F32),
+            dma((4,)), dma((4,)), dma((4,)), dma((4,)), dma((parts,)), dma((parts,)),
+            dma((len(SPANS), RS_SIB)), dma((len(SPANS), RS_SIB)), dma((2,)),
+        ],
+        compiler_params=pltpu.CompilerParams(
+            collective_id=1, has_side_effects=True, vmem_limit_bytes=48 * 1024 * 1024
+        ),
+        cost_estimate=pl.CostEstimate(flops=4_000_000_000, bytes_accessed=20_000_000, transcendentals=0),
+        name="fetch",
+    )(tokens_t, og_ext, tenant8, halves, table)
+
+
+def give_kernel(full_ref, place_ref, rows_r, leaving, landed, rows_s, psend, precv, ysend, yrecv):
+    d = lax.axis_index("dp")
+    t = lax.axis_index("tensor")
+    feat, width = full_ref.shape
+    parts = D // feat
+    barrier = pltpu.get_barrier_semaphore()
+
+    def greet(o, carry):
+        pl.semaphore_signal(
+            barrier, inc=1, device_id={"dp": d, "tensor": lax.rem(t + o, parts)}, device_id_type=MESH
+        )
+        return carry
+
+    lax.fori_loop(1, parts, greet, 0)
+    for o in (1, 2, 3):
+        pl.semaphore_signal(barrier, inc=1, device_id={"dp": lax.rem(d + o, 4), "tensor": t}, device_id_type=MESH)
+
+    place = place_ref[0:1]
+
+    def pack(there):
+        sel = (lax.broadcasted_iota(jnp.int32, (4 * SLOT, width), 0) + there * 128 == place).astype(F32).astype(BF16)
+        return nt(full_ref[...], sel).astype(BF16)
+
+    landed[t] = pack(t)
+    pl.semaphore_wait(barrier, parts - 1 + 3)
+
+    def plane_copy(there, at):
+        return pltpu.make_async_remote_copy(
+            src_ref=leaving.at[there], dst_ref=landed.at[at], send_sem=psend.at[there], recv_sem=precv.at[at],
+            device_id={"dp": d, "tensor": there}, device_id_type=MESH,
+        )
+
+    def scatter(o, carry):
+        there = lax.rem(t + o, parts)
+        leaving[there] = pack(there)
+        plane_copy(there, t).start()
+        return carry
+
+    lax.fori_loop(1, parts, scatter, 0)
+
+    group = 8
+
+    def y_copy(q, there):
+        return pltpu.make_async_remote_copy(
+            src_ref=rows_s.at[q, there], dst_ref=rows_r.at[q, d], send_sem=ysend.at[q, there], recv_sem=yrecv.at[q, d],
+            device_id={"dp": there, "tensor": t}, device_id_type=MESH,
+        )
+
+    def arrive(src):
+        @pl.when(src != t)
+        def _():
+            pltpu.make_async_remote_copy(
+                src_ref=landed.at[src], dst_ref=landed.at[src], send_sem=psend.at[src], recv_sem=precv.at[src],
+                device_id={"dp": d, "tensor": src}, device_id_type=MESH,
+            ).wait_recv()
+
+    def quarter(n, carry):
+        q = lax.rem(t // group + 4 - n, 4)
+
+        def take(i, inner):
+            arrive(q * group + i)
+            return inner
+
+        lax.fori_loop(0, group, take, 0)
+        block = landed[pl.ds(q * group, group)].reshape(group * feat, 4 * SLOT)
+        rows_s[q] = block.T.reshape(4, SLOT, group * feat)
+        for o in (1, 3, 2):
+            y_copy(q, lax.rem(d + o, 4)).start()
+        rows_r[q, d] = rows_s[q, d]
+        return carry
+
+    lax.fori_loop(0, 4, quarter, 0)
+
+    def finish(q, carry):
+        for o in (1, 3, 2):
+            there = lax.rem(d + o, 4)
+            y_copy(q, there).wait_send()
+            pltpu.make_async_remote_copy(
+                src_ref=rows_r.at[q, there], dst_ref=rows_r.at[q, there],
+                send_sem=ysend.at[q, there], recv_sem=yrecv.at[q, there],
+                device_id={"dp": there, "tensor": t}, device_id_type=MESH,
+            ).wait_recv()
+        return carry
+
+    lax.fori_loop(0, 4, finish, 0)
+
+    def drain(o, carry):
+        plane_copy(lax.rem(t + o, parts), t).wait_send()
+        return carry
+
+    lax.fori_loop(1, parts, drain, 0)
+
+
+def give(full_grad, place):
+    feat, width = full_grad.shape
+    parts = D // feat
+    vm = pl.BlockSpec(memory_space=pltpu.VMEM)
+    dma = pltpu.SemaphoreType.DMA
+    return pl.pallas_call(
+        give_kernel,
+        out_shape=jax.ShapeDtypeStruct((4, 4, SLOT, D // 4), BF16),
+        in_specs=[vm] * 2,
+        out_specs=vm,
+        scratch_shapes=[
+            pltpu.VMEM((parts, feat, 4 * SLOT), BF16),
+            pltpu.VMEM((parts, feat, 4 * SLOT), BF16),
+            pltpu.VMEM((4, 4, SLOT, D // 4), BF16),
+            dma((parts,)), dma((parts,)), dma((4, 4)), dma((4, 4)),
+        ],
+        compiler_params=pltpu.CompilerParams(
+            collective_id=2, has_side_effects=True, vmem_limit_bytes=48 * 1024 * 1024
+        ),
+        cost_estimate=pl.CostEstimate(flops=2_000_000_000, bytes_accessed=3_000_000, transcendentals=0),
+        name="give",
+    )(full_grad, place)
+
+
 def per_device(tokens_in, out_grad, tenant, slot_of, steer_table, norm_gain, w_gate, w_up, w_down):
-    holders = lax.axis_size(("dp", "tensor"))
-    groups = lax.axis_size("dp")
-    width_parts = lax.axis_size("tensor")
-    rows_own = steer_table.shape[0]
     feat_local = tokens_in.shape[1]
     token_count = tenant.shape[0]
-    capacity = 4 * token_count // holders
-    group = lax.axis_index("dp")
-    me = lax.axis_index(("dp", "tensor"))
-
-    tenant_all = lax.all_gather(tenant, "dp", axis=0, tiled=True)
     out_grad_t = out_grad.T
     gain_own = jnp.broadcast_to(norm_gain[:, None], (feat_local, 128))
-    og_ext = lax.all_gather(jnp.concatenate([out_grad_t, gain_own], axis=1), "tensor", axis=0, tiled=True)
-
-    owners_all, rows_all = look_up_slots(slot_of, tenant_all)
-    earlier = (
-        jnp.arange(token_count, dtype=jnp.int32)[:, None] < jnp.arange(token_count, dtype=jnp.int32)[None, :]
-    ).astype(BF16)
-    mine = (owners_all == me).reshape(groups, token_count)
-    rank_mine = dot(mine.astype(BF16), earlier, 1, 0).astype(jnp.int32)
-    slot_of_token = jnp.where(mine, rank_mine, -1)
-    slots = (slot_of_token[:, None, :] == jnp.arange(capacity, dtype=jnp.int32)[None, :, None]).astype(BF16)
-    row_hot = one_hot(rows_all.reshape(groups, token_count), rows_own).astype(BF16)
-    wanted = lax.dot_general(slots, row_hot, (((2,), (1,)), ((0,), (0,))), preferred_element_type=F32)
-    wanted = wanted.astype(BF16).reshape(groups * capacity, rows_own)
-    picked = dot(wanted, steer_table, 1, 0).astype(BF16)
-    outgoing = picked.reshape(groups, capacity, width_parts, feat_local).transpose(0, 2, 1, 3)
-    outgoing = outgoing.reshape(holders, capacity, feat_local)
-    returned = lax.all_to_all(outgoing, ("dp", "tensor"), split_axis=0, concat_axis=0, tiled=True)
-    returned = returned.reshape(holders * capacity, feat_local)
-
-    owners = lax.dynamic_slice_in_dim(owners_all, group * token_count, token_count)
-    matches = one_hot(owners, holders).astype(BF16)
-    before = dot(earlier, matches, 0, 0)
-    ranking = jnp.sum(jnp.where(matches > 0, before, 0.0), axis=1).astype(jnp.int32)
-    place = one_hot(owners * capacity + ranking, holders * capacity).astype(BF16)
-    steering = dot(returned, place, 0, 1)
-
-    residual = (tokens_in.T.astype(F32) + steering).astype(BF16)
+    lines = slot_of.reshape(-1, 128).T
+    halves = jnp.concatenate([lines // 256, lines % 256], axis=0).astype(BF16)
+    tenant8 = jnp.broadcast_to(tenant[None, :], (8, token_count))
+    residual, og_ext, wanted, place = fetch(
+        tokens_in.T, jnp.concatenate([out_grad_t, gain_own], axis=1), tenant8, halves, steer_table
+    )
+    og_ext = og_ext.reshape(D, token_count + 128)
     full_grad = core(residual, out_grad_t, gain_own, og_ext, w_down, w_gate, w_up)
-
-    sending = dot(place, full_grad, 0, 1).astype(BF16).reshape(holders, capacity, feat_local)
-    received = lax.all_to_all(sending, ("dp", "tensor"), split_axis=0, concat_axis=0, tiled=True)
-    received = received.reshape(groups, width_parts, capacity, feat_local).transpose(0, 2, 1, 3)
-    received = received.reshape(groups * capacity, width_parts * feat_local)
-    table_grad = dot(wanted, received, 0, 0)
+    rows = give(full_grad, place)
+    rows = rows.transpose(1, 2, 0, 3).reshape(4 * SLOT, D)
+    table_grad = lax.dot_general(wanted, rows, (((0,), (0,)), ((), ())), preferred_element_type=F32)
     return (full_grad.T, table_grad)
 
 

time: 231 us -> 222 us (0.961)
  Pallas kernels: 78.9 us -> 192 us
  waiting for transfers between devices: 47.6 us -> 0 us
  starting transfers between devices: 24.2 us -> 0 us
  between operations: 14.2 us -> 0.74 us
  matrix products: 16.4 us -> 3.23 us
  local copies, waits for them, and re-layouts: 35.5 us -> 24.3 us
  blocking collectives: 10.3 us -> 0 us
    pallas_call x0 -> x2, Pallas kernels: none -> 105 us  [the longest x1 60.3 us: fetch(): pl.pallas_call(fetch_kernel, out_shape=(jax.ShapeDtypeStruct((feat, width...]
    all_to_all x2 -> x0, waiting for transfers between devices: 47.6 us -> none  [the longest x1 24.4 us: per_device(): lax.all_to_all(sending, ('dp', 'tensor'), split_axis=0, concat_axis=0, ti...]
    all_to_all x2 -> x0, starting transfers between devices: 24.1 us -> none  [the longest x1 13.2 us: per_device(): lax.all_to_all(outgoing, ('dp', 'tensor'), split_axis=0, concat_axis=0, t...]
    reshape x4 -> x1, local copies, waits for them, and re-layouts: 14.6 us -> 1 us  [per_device(): lines = slot_of.reshape(-1, 128).T]
    dot_general x8 -> x1, matrix products: 16.4 us -> 3.23 us  [per_device(): lax.dot_general(wanted, rows, (((0,), (0,)), ((), ())), preferred_element...]
    all_gather x1 -> x0, blocking collectives: 10.3 us -> none  [per_device(): tenant_all = lax.all_gather(tenant, 'dp', axis=0, tiled=True)]
    pallas_call x1, Pallas kernels: 78.9 us -> 86.9 us  [core(): pl.pallas_call(core_kernel, out_shape=jax.ShapeDtypeStruct(residual.shape...]
    unnamed x12 -> x14, local copies, waits for them, and re-layouts: 17.4 us -> 20.9 us
  transfers between devices with their start and end apart: 3 -> 0, of which waited for: 2 -> 0; matrix products, arithmetic and copies ran while one was open for 15% -> 0% of each run, Pallas kernels for 0% -> 0%
where the time goes in v1:
time: 222 us
  Pallas kernels  192 us (86%)
  local copies, waits for them, and re-layouts  24.3 us (11%)
  matrix products  3.23 us (1%)
    pallas_call x1, Pallas kernels, core(): pl.pallas_call(core_kernel, out_shape=jax.ShapeDtypeStruct(residual.shape...  86.9 us
    pallas_call x1, Pallas kernels, fetch(): pl.pallas_call(fetch_kernel, out_shape=(jax.ShapeDtypeStruct((feat, width...  60.3 us
    pallas_call x1, Pallas kernels, give(): pl.pallas_call(give_kernel, out_shape=jax.ShapeDtypeStruct((4, 4, SLOT, D...  45.1 us
    unnamed x14, local copies, waits for them, and re-layouts  20.9 us

profile of v1, /device:TPU:1, one launch (start us, length us, event | category | flops | bytes accessed | tf_op | source)
XLA Modules:
  0.0 221.7 jit_solution(6441879614526960644)
XLA Ops:
  0.6 1.0 copy.13
  1.6 0.1 fusion
  1.8 0.7 broadcast_in_dim.4.gain_own_ref
  2.5 0.0 copy-start.4
  2.5 1.0 pad_maximum_fusion.og_ref
  3.5 0.7 broadcast_in_dim.5.ten_ref
  4.2 0.0 copy-start.1
  4.2 1.7 copy-done.1
  6.0 0.0 copy-start.2
  6.0 0.9 copy-done.2
  6.9 60.3 %fetch.1 = (bf16[160,768]{1,0:T(8,128)(2,1)S(1)}, bf16[4,4,2,2,80,896]{5,4,3,2,1,0:T(8,128)(2,1)}, bf16[128,256]{1,0:T(8,128)(2,1)S(1)}, s32[8,768]{1,0:T(8,128)S(1)}) custom-call(bf16[160,768]{1,0:T(8,128)(2,1)S(1)} %bitcast.41, bf16[160,896]{1,0:T(8,128)(2,1)S(1)} %pad_maximum_fusion.og_ref, s32[8,768]{1,0:T(8,128)S(1)} %broadcast_in_dim.5.ten_ref, ...), custom_call_target="tpu_custom_call" | custom-call | flops 4000000000 | bytes 20000000 | tf_op jit(solution)/shard_map/fetch/pallas_call | solution.py:640
  67.2 0.0 copy-done.4
  67.2 0.0 copy-start.3
  67.2 0.7 copy-done.3
  67.9 7.9 %copy.14 = bf16[5120,512]{0,1:T(8,128)(2,1)} copy(bf16[5120,512]{1,0:T(8,128)(2,1)} %wg_hbm.1) | data formatting | bytes 10485760 | tf_op args[6]
  75.8 7.8 %copy.15 = bf16[5120,512]{0,1:T(8,128)(2,1)} copy(bf16[5120,512]{1,0:T(8,128)(2,1)} %wu_hbm.1) | data formatting | bytes 10485760 | tf_op args[7]
  83.6 86.9 %core.1.full_ref = bf16[160,768]{1,0:T(8,128)(2,1)} custom-call(bf16[160,768]{1,0:T(8,128)(2,1)} %copy-done.3, bf16[160,768]{1,0:T(8,128)(2,1)} %bitcast.47, bf16[160,128]{1,0:T(8,128)(2,1)} %copy-done.4, bf16[5120,896]{1,0:T(8,128)(2,1)} %bitcast.49, bf16[512,5120]{1,0:T(8,128)(2,1)} %wd_hbm.1, bf16[5120,512]{1,0:T(8,128)(2,1)} %wg_hbm.1, ...), custom_call_target="tpu_custom_call" | custom-call | flops 20132659200 | bytes 40000000 | tf_op jit(solution)/shard_map/core/pallas_call | solution.py:354
  170.6 0.0 copy-start
  170.6 0.9 copy-done
  171.5 45.1 %give.1 = bf16[4,4,32,1280]{3,2,1,0:T(8,128)(2,1)S(1)} custom-call(bf16[160,768]{1,0:T(8,128)(2,1)S(1)} %copy-done, s32[8,768]{1,0:T(8,128)S(1)} %get-tuple-element.9.place_ref), custom_call_target="tpu_custom_call" | custom-call | flops 2000000000 | bytes 3000000 | tf_op jit(solution)/shard_map/give/pallas_call | solution.py:767
  216.6 1.0 copy.16
  217.7 0.2 copy.17
  217.8 3.2 %fusion.5 = f32[256,5120]{1,0:T(8,128)} fusion(bf16[128,256]{1,0:T(8,128)(2,1)S(1)} %get-tuple-element.8, bf16[128,5120]{1,0:T(8,128)(2,1)S(1)} %bitcast.42), kind=kOutput, calls=%fused_computation.14 | convolution fusion | flops 335544320 | bytes 6619136 | tf_op jit(solution)/shard_map/dot_general | solution.py:801
  221.1 0.7 copy.19
  (1 shorter events, 0.0 us)
Async XLA Ops:
  2.5 64.7 %copy-start.4 = (bf16[160,128]{1,0:T(8,128)(2,1)}, bf16[160,128]{1,0:T(8,128)(2,1)S(1)}, u32[]{:S(2)}) copy-start(bf16[160,128]{1,0:T(8,128)(2,1)S(1)} %broadcast_in_dim.4.gain_own_ref) | copy-start | bytes 122884
  4.2 1.7 copy-start.1
  6.0 0.9 copy-start.2
  67.2 0.7 copy-start.3
  170.6 0.9 copy-start

commit v2 on v1

--- a/solution.py
+++ b/solution.py
@@ -337,7 +337,7 @@
         copy.wait_send()
 
 
-def core(residual, out_grad_t, gain_own, og_ext, w_down, w_gate, w_up):
+def core(residual, out_grad_t, gain_own, og_ext, w_down, w_gate, w_up, w_gate_t, w_up_t):
     width = residual.shape[1]
     tok = width // CHUNKS
     hid = w_gate.shape[1]
@@ -379,7 +379,7 @@
         ),
         cost_estimate=pl.CostEstimate(flops=10 * D * hid * width, bytes_accessed=40_000_000, transcendentals=0),
         name="core",
-    )(residual, out_grad_t, gain_own, og_ext, w_down, w_gate, w_up, w_gate.T, w_up.T)
+    )(residual, out_grad_t, gain_own, og_ext, w_down, w_gate, w_up, w_gate_t, w_up_t)
 
 
 MESH = pl.DeviceIdType.MESH
@@ -392,9 +392,9 @@
 
 
 def fetch_kernel(
-    tok_ref, og_ref, ten_ref, halves_ref, table_ref,
-    res_ref, og_out, wanted_ref, place_ref,
-    tbuf, earlier, rows_s, rows_r, turned, landed, acc,
+    tok_ref, og_ref, ten_ref, halves_ref, table_ref, wg_hbm, wu_hbm,
+    res_ref, og_out, wanted_ref, place_ref, wgt_hbm, wut_hbm,
+    tbuf, earlier, rows_s, rows_r, turned, landed, acc, w_buf, wt_buf,
     tsend, trecv, ysend, yrecv, psend, precv, gsend, grecv, lsem,
 ):
     d = lax.axis_index("dp")
@@ -421,6 +421,10 @@
         pltpu.make_async_copy(og_ref.at[pl.ds(h * HALF, HALF)], og_out.at[x, z, c, h], lsem.at[h]) for h in range(2)
     ]
     for copy in own_copies:
+        copy.start()
+    w_in = [pltpu.make_async_copy(src, w_buf.at[n], lsem.at[2 + n]) for n, src in enumerate((wg_hbm, wu_hbm))]
+    w_out = [pltpu.make_async_copy(wt_buf.at[n], dst, lsem.at[4 + n]) for n, dst in enumerate((wgt_hbm, wut_hbm))]
+    for copy in w_in:
         copy.start()
     barrier = pltpu.get_barrier_semaphore()
 
@@ -558,84 +562,130 @@
         slot = jnp.where(mine > 0, before.astype(jnp.int32), -1)
         wanted = nt(hot(slot, SLOT).astype(BF16), hot(row, table_ref.shape[0]).astype(BF16)).astype(BF16)
         wanted_ref[g * SLOT:(g + 1) * SLOT] = wanted
-        rows_s[g] = jnp.dot(wanted, table_ref[...], preferred_element_type=F32).astype(BF16)
-    for o in (1, 3, 2):
-        there = lax.rem(d + o, 4)
-        send(rows_s.at[there], rows_r.at[d], ysend.at[there], yrecv.at[d], {"dp": there, "tensor": t})
-    rows_r[d] = rows_s[d]
+
+    quarter = D // 4
+
+    def y_copy(q, there, at):
+        return pltpu.make_async_remote_copy(
+            src_ref=rows_s.at[q, there], dst_ref=rows_r.at[q, at], send_sem=ysend.at[q, there], recv_sem=yrecv.at[q, at],
+            device_id={"dp": there, "tensor": t}, device_id_type=MESH,
+        )
+
+    others = tuple(lax.rem(d + o, 4) for o in (1, 3, 2))
+    order = (x, lax.rem(x + 1, 4), lax.rem(x + 3, 4), xo)
+
+    def pick(q):
+        cols = pl.ds(pl.multiple_of(q * quarter, quarter), quarter)
+        picked = jnp.dot(wanted_ref[...], table_ref[:, cols], preferred_element_type=F32)
+        rows_s[q] = picked.astype(BF16).reshape(4, SLOT, quarter)
+        for there in others:
+            y_copy(q, there, d).start()
+        rows_r[q, d] = rows_s[q, d]
+
+    for q in order:
+        pick(q)
     for copy in own_copies:
         copy.wait()
     ag3(0)
     ag3(1)
+
+    def turn_weight(n):
+        w_in[n].wait()
+        wide = 640
+
+        def body(i, carry):
+            at = pl.multiple_of(i * wide, wide)
+            wt_buf[n, :, pl.ds(at, wide)] = w_buf[n, pl.ds(at, wide), :].T
+            return carry
+
+        lax.fori_loop(0, D // wide, body, 0)
+        w_out[n].start()
+
+    def plane_copy(there):
+        return pltpu.make_async_remote_copy(
+            src_ref=turned.at[there], dst_ref=landed.at[t], send_sem=psend.at[there], recv_sem=precv.at[t],
+            device_id={"dp": d, "tensor": there}, device_id_type=MESH,
+        )
+
+    row = parts // 4
+
+    def pass_on(n):
+        q = order[n]
+        for there in others:
+            pltpu.make_async_remote_copy(
+                src_ref=rows_r.at[q, there], dst_ref=rows_r.at[q, there],
+                send_sem=ysend.at[q, there], recv_sem=yrecv.at[q, there],
+                device_id={"dp": there, "tensor": t}, device_id_type=MESH,
+            ).wait_recv()
+        turned[pl.ds(q * row, row)] = rows_r[q].reshape(4 * SLOT, quarter).T.reshape(row, feat, 4 * SLOT)
+
+        def scatter(i, carry):
+            plane_copy(q * row + lax.rem(lax.rem(t, row) + i, row)).start()
+            return carry
+
+        lax.fori_loop(1 if n == 0 else 0, row, scatter, 0)
+        if n == 0:
+            landed[t] = turned[t]
+
+    turn_weight(0)
+    pass_on(0)
     ag4(0)
-    for o in (3, 1, 2):
-        there = lax.rem(d + o, 4)
-        got(rows_r.at[there], ysend.at[there], yrecv.at[there], {"dp": there, "tensor": t})
-    wide = 640
-
-    def turn(i, carry):
-        at = pl.multiple_of(i * wide, wide)
-        block = rows_r[:, :, pl.ds(at, wide)].reshape(4 * SLOT, wide)
-        turned[pl.ds(at, wide), :] = block.T
-        return carry
-
-    lax.fori_loop(0, D // wide, turn, 0)
-
-    def scatter(o, carry):
-        there = lax.rem(t + o, parts)
-        pltpu.make_async_remote_copy(
-            src_ref=turned.at[pl.ds(pl.multiple_of(there * feat, 16), feat)], dst_ref=landed.at[t],
-            send_sem=psend.at[there], recv_sem=precv.at[t],
-            device_id={"dp": d, "tensor": there}, device_id_type=MESH,
-        ).start()
-        return carry
-
-    lax.fori_loop(1, parts, scatter, 0)
-    landed[t] = turned[pl.ds(pl.multiple_of(t * feat, 16), feat), :]
+    pass_on(1)
+    pass_on(2)
+    pass_on(3)
     acc[...] = tok_ref[...].astype(F32)
+    turn_weight(1)
     ag4(1)
     ag5(0)
 
-    def add_from(src):
-        sel = (lax.broadcasted_iota(jnp.int32, (128, width), 0) + src * 128 == place).astype(F32).astype(BF16)
-        acc[...] += jnp.dot(landed[src], sel, preferred_element_type=F32)
-
-    add_from(t)
-
-    def gather(o, carry):
-        src = lax.rem(t + parts - o, parts)
-        pltpu.make_async_remote_copy(
-            src_ref=landed.at[src], dst_ref=landed.at[src],
-            send_sem=psend.at[src], recv_sem=precv.at[src],
-            device_id={"dp": d, "tensor": src}, device_id_type=MESH,
-        ).wait_recv()
-        add_from(src)
+    def arrive(src):
+        @pl.when(src != t)
+        def _():
+            pltpu.make_async_remote_copy(
+                src_ref=landed.at[src], dst_ref=landed.at[src], send_sem=psend.at[src], recv_sem=precv.at[src],
+                device_id={"dp": d, "tensor": src}, device_id_type=MESH,
+            ).wait_recv()
+
+    def gather(q):
+        def body(i, carry):
+            pair = q * (row // 2) + i
+            arrive(2 * pair)
+            arrive(2 * pair + 1)
+            sel = (lax.broadcasted_iota(jnp.int32, (256, width), 0) + pair * 256 == place).astype(F32).astype(BF16)
+            both = jnp.concatenate([landed[2 * pair], landed[2 * pair + 1]], axis=1)
+            acc[...] += jnp.dot(both, sel, preferred_element_type=F32)
+            return carry
+
+        lax.fori_loop(0, row // 2, body, 0)
+
+    gather(x)
+    ag5(1)
+    gather(order[2])
+    gather(order[1])
+    ag6(0)
+    gather(xo)
+    res_ref[...] = acc[...].astype(BF16)
+    ag6(1)
+
+    def drain(o, carry):
+        plane_copy(lax.rem(t + o, parts)).wait_send()
         return carry
 
-    lax.fori_loop(1, parts, gather, 0)
-    res_ref[...] = acc[...].astype(BF16)
-    ag5(1)
-    ag6(0)
-    ag6(1)
-
-    def drain(o, carry):
-        there = lax.rem(t + o, parts)
-        pltpu.make_async_remote_copy(
-            src_ref=turned.at[pl.ds(pl.multiple_of(there * feat, 16), feat)], dst_ref=landed.at[t],
-            send_sem=psend.at[there], recv_sem=precv.at[t],
-            device_id={"dp": d, "tensor": there}, device_id_type=MESH,
-        ).wait_send()
-        return carry
-
     lax.fori_loop(1, parts, drain, 0)
+    for q in range(4):
+        for there in others:
+            y_copy(q, there, d).wait_send()
     for copy in sent:
         copy.wait_send()
-
-
-def fetch(tokens_t, og_ext, tenant8, halves, table):
+    for copy in w_out:
+        copy.wait()
+
+
+def fetch(tokens_t, og_ext, tenant8, halves, table, w_gate, w_up):
     feat, width = tokens_t.shape
     parts = D // feat
     vm = pl.BlockSpec(memory_space=pltpu.VMEM)
+    hbm = pl.BlockSpec(memory_space=pl.ANY)
     dma = pltpu.SemaphoreType.DMA
     return pl.pallas_call(
         fetch_kernel,
@@ -644,26 +694,30 @@
             jax.ShapeDtypeStruct((SIDE, SIDE, 2, 2, HALF, og_ext.shape[1]), BF16),
             jax.ShapeDtypeStruct((4 * SLOT, table.shape[0]), BF16),
             jax.ShapeDtypeStruct((8, width), jnp.int32),
+            jax.ShapeDtypeStruct(w_gate.shape[::-1], BF16),
+            jax.ShapeDtypeStruct(w_up.shape[::-1], BF16),
         ),
-        in_specs=[vm] * 5,
-        out_specs=(vm, pl.BlockSpec(memory_space=pl.ANY), vm, vm),
+        in_specs=[vm] * 5 + [hbm] * 2,
+        out_specs=(vm, hbm, vm, vm, hbm, hbm),
         scratch_shapes=[
             pltpu.VMEM((4, 8, width), jnp.int32),
             pltpu.VMEM((width, width), BF16),
-            pltpu.VMEM((4, SLOT, D), BF16),
-            pltpu.VMEM((4, SLOT, D), BF16),
-            pltpu.VMEM((D, 4 * SLOT), BF16),
+            pltpu.VMEM((4, 4, SLOT, D // 4), BF16),
+            pltpu.VMEM((4, 4, SLOT, D // 4), BF16),
+            pltpu.VMEM((parts, feat, 4 * SLOT), BF16),
             pltpu.VMEM((parts, feat, 4 * SLOT), BF16),
             pltpu.VMEM((feat, width), F32),
-            dma((4,)), dma((4,)), dma((4,)), dma((4,)), dma((parts,)), dma((parts,)),
-            dma((len(SPANS), RS_SIB)), dma((len(SPANS), RS_SIB)), dma((2,)),
+            pltpu.VMEM((2,) + w_gate.shape, BF16),
+            pltpu.VMEM((2,) + w_gate.shape[::-1], BF16),
+            dma((4,)), dma((4,)), dma((4, 4)), dma((4, 4)), dma((parts,)), dma((parts,)),
+            dma((len(SPANS), RS_SIB)), dma((len(SPANS), RS_SIB)), dma((6,)),
         ],
         compiler_params=pltpu.CompilerParams(
             collective_id=1, has_side_effects=True, vmem_limit_bytes=48 * 1024 * 1024
         ),
         cost_estimate=pl.CostEstimate(flops=4_000_000_000, bytes_accessed=20_000_000, transcendentals=0),
         name="fetch",
-    )(tokens_t, og_ext, tenant8, halves, table)
+    )(tokens_t, og_ext, tenant8, halves, table, w_gate, w_up)
 
 
 def give_kernel(full_ref, place_ref, rows_r, leaving, landed, rows_s, psend, precv, ysend, yrecv):
@@ -684,12 +738,6 @@
         pl.semaphore_signal(barrier, inc=1, device_id={"dp": lax.rem(d + o, 4), "tensor": t}, device_id_type=MESH)
 
     place = place_ref[0:1]
-
-    def pack(there):
-        sel = (lax.broadcasted_iota(jnp.int32, (4 * SLOT, width), 0) + there * 128 == place).astype(F32).astype(BF16)
-        return nt(full_ref[...], sel).astype(BF16)
-
-    landed[t] = pack(t)
     pl.semaphore_wait(barrier, parts - 1 + 3)
 
     def plane_copy(there, at):
@@ -698,13 +746,38 @@
             device_id={"dp": d, "tensor": there}, device_id_type=MESH,
         )
 
-    def scatter(o, carry):
-        there = lax.rem(t + o, parts)
-        leaving[there] = pack(there)
-        plane_copy(there, t).start()
+    def pack(pair):
+        sel = (lax.broadcasted_iota(jnp.int32, (256, width), 0) + pair * 256 == place).astype(F32).astype(BF16)
+        packed = nt(full_ref[...], sel).astype(BF16)
+        for half in range(2):
+            there = 2 * pair + half
+            leaving[there] = packed[:, 128 * half:128 * half + 128]
+
+            @pl.when(there != t)
+            def _():
+                plane_copy(there, t).start()
+
+    quad = parts // 8
+    x = t // 8
+
+    def own_row(i, carry):
+        pack(x * quad + lax.rem(lax.rem(t // 2, quad) + i, quad))
         return carry
 
-    lax.fori_loop(1, parts, scatter, 0)
+    def side_rows(i, carry):
+        at = lax.rem(lax.rem(t // 2, quad) + i, quad)
+        pack(lax.rem(x + 1, 4) * quad + at)
+        pack(lax.rem(x + 3, 4) * quad + at)
+        return carry
+
+    def far_row(i, carry):
+        pack(lax.rem(x + 2, 4) * quad + lax.rem(lax.rem(t // 2, quad) + i, quad))
+        return carry
+
+    lax.fori_loop(0, quad, own_row, 0)
+    landed[t] = leaving[t]
+    lax.fori_loop(0, quad, side_rows, 0)
+    lax.fori_loop(0, quad, far_row, 0)
 
     group = 8
 
@@ -722,8 +795,7 @@
                 device_id={"dp": d, "tensor": src}, device_id_type=MESH,
             ).wait_recv()
 
-    def quarter(n, carry):
-        q = lax.rem(t // group + 4 - n, 4)
+    for q in (x, lax.rem(x + 3, 4), lax.rem(x + 1, 4), lax.rem(x + 2, 4)):
 
         def take(i, inner):
             arrive(q * group + i)
@@ -735,9 +807,6 @@
         for o in (1, 3, 2):
             y_copy(q, lax.rem(d + o, 4)).start()
         rows_r[q, d] = rows_s[q, d]
-        return carry
-
-    lax.fori_loop(0, 4, quarter, 0)
 
     def finish(q, carry):
         for o in (1, 3, 2):
@@ -791,11 +860,11 @@
     lines = slot_of.reshape(-1, 128).T
     halves = jnp.concatenate([lines // 256, lines % 256], axis=0).astype(BF16)
     tenant8 = jnp.broadcast_to(tenant[None, :], (8, token_count))
-    residual, og_ext, wanted, place = fetch(
-        tokens_in.T, jnp.concatenate([out_grad_t, gain_own], axis=1), tenant8, halves, steer_table
+    residual, og_ext, wanted, place, w_gate_t, w_up_t = fetch(
+        tokens_in.T, jnp.concatenate([out_grad_t, gain_own], axis=1), tenant8, halves, steer_table, w_gate, w_up
     )
     og_ext = og_ext.reshape(D, token_count + 128)
-    full_grad = core(residual, out_grad_t, gain_own, og_ext, w_down, w_gate, w_up)
+    full_grad = core(residual, out_grad_t, gain_own, og_ext, w_down, w_gate, w_up, w_gate_t, w_up_t)
     rows = give(full_grad, place)
     rows = rows.transpose(1, 2, 0, 3).reshape(4 * SLOT, D)
     table_grad = lax.dot_general(wanted, rows, (((0,), (0,)), ((), ())), preferred_element_type=F32)

time: 222 us -> 192 us (0.86)
  local copies, waits for them, and re-layouts: 24.3 us -> 8.63 us
  Pallas kernels: 192 us -> 178 us
    unnamed x14 -> x12, local copies, waits for them, and re-layouts: 20.9 us -> 5.17 us
    pallas_call x1, Pallas kernels: 86.9 us -> 79.1 us  [core(): pl.pallas_call(core_kernel, out_shape=jax.ShapeDtypeStruct(residual.shape...]
    pallas_call x1, Pallas kernels: 60.3 us -> 55.6 us  [fetch(): pl.pallas_call(fetch_kernel, out_shape=(jax.ShapeDtypeStruct((feat, width...]
    pallas_call x1, Pallas kernels: 45.1 us -> 42.8 us  [give(): pl.pallas_call(give_kernel, out_shape=jax.ShapeDtypeStruct((4, 4, SLOT, D...]
where the time goes in v2:
time: 192 us; the launch traced here: 191 us
  Pallas kernels  178 us (93%)
  local copies, waits for them, and re-layouts  8.63 us (4%)
  matrix products  3.22 us (2%)
    pallas_call x1, Pallas kernels, core(): pl.pallas_call(core_kernel, out_shape=jax.ShapeDtypeStruct(residual.shape...  79.1 us
    pallas_call x1, Pallas kernels, fetch(): pl.pallas_call(fetch_kernel, out_shape=(jax.ShapeDtypeStruct((feat, width...  55.6 us
    pallas_call x1, Pallas kernels, give(): pl.pallas_call(give_kernel, out_shape=jax.ShapeDtypeStruct((4, 4, SLOT, D...  42.8 us
    unnamed x12, local copies, waits for them, and re-layouts  5.17 us

profile of v2, /device:TPU:1, one launch (start us, length us, event | category | flops | bytes accessed | tf_op | source)
XLA Modules:
  0.0 191.2 jit_solution(4953646821752715675)
XLA Ops:
  0.6 0.7 broadcast_in_dim.5.ten_ref
  1.3 0.7 broadcast_in_dim.4.gain_own_ref
  2.1 0.0 copy-start.4
  2.1 1.0 copy.11
  3.1 0.1 fusion
  3.3 1.0 pad_maximum_fusion.og_ref
  4.2 0.0 copy-start.1
  4.2 1.7 copy-done.1
  6.0 0.0 copy-start.2
  6.0 0.9 copy-done.2
  6.9 55.6 %fetch.1 = (bf16[160,768]{1,0:T(8,128)(2,1)S(1)}, bf16[4,4,2,2,80,896]{5,4,3,2,1,0:T(8,128)(2,1)}, bf16[128,256]{1,0:T(8,128)(2,1)S(1)}, s32[8,768]{1,0:T(8,128)...) custom-call(bf16[160,768]{1,0:T(8,128)(2,1)S(1)} %bitcast.39, bf16[160,896]{1,0:T(8,128)(2,1)S(1)} %pad_maximum_fusion.og_ref, ...), custom_call_target="tpu_custom_call" | custom-call | flops 4000000000 | bytes 20000000 | tf_op jit(solution)/shard_map/fetch/pallas_call | solution.py:690
  62.5 0.0 copy-done.4
  62.6 0.0 copy-start.3
  62.6 0.7 copy-done.3
  63.2 79.1 %core.1.full_ref = bf16[160,768]{1,0:T(8,128)(2,1)} custom-call(bf16[160,768]{1,0:T(8,128)(2,1)} %copy-done.3, bf16[160,768]{1,0:T(8,128)(2,1)} %bitcast.43, bf16[160,128]{1,0:T(8,128)(2,1)} %copy-done.4, bf16[5120,896]{1,0:T(8,128)(2,1)} %bitcast.45, bf16[512,5120]{1,0:T(8,128)(2,1)} %wd_hbm.1, bf16[5120,512]{1,0:T(8,128)(2,1)} %wg_hbm.3, ...), custom_call_target="tpu_custom_call" | custom-call | flops 20132659200 | bytes 40000000 | tf_op jit(solution)/shard_map/core/pallas_call | solution.py:354
  142.4 0.0 copy-start
  142.4 0.9 copy-done
  143.3 42.8 %give.1 = bf16[4,4,32,1280]{3,2,1,0:T(8,128)(2,1)S(1)} custom-call(bf16[160,768]{1,0:T(8,128)(2,1)S(1)} %copy-done, s32[8,768]{1,0:T(8,128)S(1)} %get-tuple-element.13.place_ref), custom_call_target="tpu_custom_call" | custom-call | flops 2000000000 | bytes 3000000 | tf_op jit(solution)/shard_map/give/pallas_call | solution.py:836
  186.1 1.0 copy.12
  187.1 0.2 copy.13
  187.3 3.2 %fusion.5 = f32[256,5120]{1,0:T(8,128)} fusion(bf16[128,256]{1,0:T(8,128)(2,1)S(1)} %get-tuple-element.12, bf16[128,5120]{1,0:T(8,128)(2,1)S(1)} %bitcast.40), kind=kOutput, calls=%fused_computation.14 | convolution fusion | flops 335544320 | bytes 6619136 | tf_op jit(solution)/shard_map/dot_general | solution.py:870
  190.5 0.7 copy.15
  (1 shorter events, 0.0 us)
Async XLA Ops:
  2.1 60.5 %copy-start.4 = (bf16[160,128]{1,0:T(8,128)(2,1)}, bf16[160,128]{1,0:T(8,128)(2,1)S(1)}, u32[]{:S(2)}) copy-start(bf16[160,128]{1,0:T(8,128)(2,1)S(1)} %broadcast_in_dim.4.gain_own_ref) | copy-start | bytes 122884
  4.2 1.7 copy-start.1
  6.0 0.9 copy-start.2
  62.6 0.7 copy-start.3
  142.4 0.9 copy-start
